TPU v7x, 256 devices: a whole 4x4x8 slice. The times are simulated.
256 devices in a mesh: site: 4 (over y), sector: 64 (over x, z, core).
Axes of the slice: x: 4, y: 4, z: 8, core: 2. Of those that a mesh axis runs over, the one named last changes fastest.
Arguments:
- env_in: bfloat16 [2, 64, 512, 512], P(None, 'sector'), may hold values from -6 to 6
- bra: bfloat16 [4, 4, 64, 512, 512], P('site', None, 'sector'), may hold values from -0.25 to 0.25
- ket: bfloat16 [4, 2, 4, 64, 512, 512], P('site', None, None, 'sector'), may hold values from -0.125 to 0.125
- sector_dims: int32 [5, 64], replicated, may hold values from 384 to 512, as said below
- flags: int32 [4, 4, 64], P('site', None, 'sector'), may hold values 0 or 1
Outputs:
- env_after: bfloat16 [4, 2, 64, 512, 512], P('site', None, 'sector')
Inputs may be any that keep to these rules, and one draw needn't show every extreme that they name: `sector_dims`: every bond has some sector whose used size is exactly 512.
All inputs are finite; a program needn't handle non-finite values. No bound on the sum of `flags` on one device may be relied on, other than what follows from the above.
Results may differ from a plain program's by a relative error of at most 0.013.
Values may be sent and summed in bfloat16 or wider, within the bound.
A program may use at most 64 MiB of HBM per device.

v0:
```python
import jax
import jax.numpy as jnp
from jax import lax
from jax.sharding import PartitionSpec as P


def shifted(array, axis, by):
    count = lax.axis_size(axis)
    pairs = [(i, i + by) for i in range(count) if 0 <= i + by < count]
    return lax.ppermute(array, axis, pairs)


def per_device(env_in, bra, ket, sector_dims, flags):
    sections = lax.axis_size("site")
    section = lax.axis_index("site")
    sector = lax.axis_index("sector")
    pairs = ket.shape[1]
    width = ket.shape[-1]
    lanes = jnp.arange(width)
    dims_here = lax.dynamic_index_in_dim(sector_dims, sector, 1, keepdims=False)
    keep_first = (lanes < dims_here[0]).astype(jnp.float32)
    first_window = keep_first[:, None] * keep_first[None, :]
    dim_next = lax.dynamic_index_in_dim(dims_here, section + 1, 0, keepdims=False)
    keep_next = (lanes < dim_next).astype(jnp.float32)
    next_window = keep_next[:, None] * keep_next[None, :]
    bra_here = bra[0, :, 0]
    ket_here = ket[0, :, :, 0]
    flag_here = flags[0, :, 0].astype(jnp.float32)

    def advance(step, carry):
        held, result = carry
        pair = step - section
        valid = jnp.logical_and(pair >= 0, pair < pairs)
        chosen = jnp.clip(pair, 0, pairs - 1)
        entering = lax.dynamic_index_in_dim(
            env_in, jnp.minimum(step, pairs - 1), 0, keepdims=False
        )[0]
        entering = (entering.astype(jnp.float32) * first_window).astype(jnp.bfloat16)
        current = jnp.where(section == 0, entering, held)
        kets = lax.dynamic_index_in_dim(ket_here, chosen, 0, keepdims=False)
        moved = jnp.einsum("ab,sbc->sac", current, kets, preferred_element_type=jnp.float32).astype(
            jnp.bfloat16
        )
        parts = (
            jnp.einsum("sba,sbc->sac", bra_here, moved, preferred_element_type=jnp.float32)
            * flag_here[:, None, None]
        )
        arrived = shifted(parts[1:3], "sector", 1)
        single = arrived[0] + arrived[1]
        double = shifted(parts[3], "sector", 2)
        total = (parts[0] + single + double) * next_window
        fresh = total.astype(jnp.bfloat16)
        updated = lax.dynamic_update_index_in_dim(result, fresh[None], chosen, 0)
        result = jnp.where(valid, updated, result)
        held = shifted(fresh, "site", 1)
        return (held, result)

    held_start = jnp.zeros((width, width), jnp.bfloat16)
    result_start = jnp.zeros((pairs, 1, width, width), jnp.bfloat16)
    held_end, result_end = lax.fori_loop(
        0, pairs + sections - 1, advance, (held_start, result_start)
    )
    return result_end[None]


def solution(mesh):
    in_specs = (
        P(None, "sector", None, None),
        P("site", None, "sector", None, None),
        P("site", None, None, "sector", None, None),
        P(),
        P("site", None, "sector"),
    )
    out_specs = P("site", None, "sector", None, None)
    return jax.shard_map(
        per_device, mesh=mesh, in_specs=in_specs, out_specs=out_specs, check_vma=False
    )
```

profile of v0, /device:TPU:23, one launch (start us, length us, event | category | flops | bytes accessed | tf_op | source)
XLA Modules:
  0.0 370.2 jit_solution(13181587639949841957)
XLA Ops:
  6.3 363.9 %while.17 = (s32[]{:T(128)}, bf16[512,512]{0,1:T(8,128)(2,1)}, bf16[2,1,512,512]{3,2,0,1:T(8,128)(2,1)}, s32[]{:T(128)}, bf16[2,4,512,512]{3,2,1,0:T(8,128)(2,1)...) while((s32[]{:T(128)}, bf16[512,512]{0,1:T(8,128)(2,1)}, ...), condition=%wide.region_1.2_spmd.clone, body=%wide.region_0.1_spmd.clone.sunk | while | flops 2152726528 | bytes 42476916 | solution.py:60
  7.6 6.8 %multiply_bitcast_fusion.2 = f32[4,512,512]{1,2,0:T(8,128)} fusion(bf16[4,512,512]{2,1,0:T(8,128)(2,1)} %get-tuple-element.390, f32[4]{0:T(128)S(1)} %get-tuple-element.391, bf16[2,4,512,512]{3,2,1,0:T(8,128)(2,1)} %get-tuple-element.387, s32[]{:T(128)S(6)} %min.21, bf16[512,512]{0,1:T(8,128)(2,1)} %get-tuple-element.370, ...), kind=kOutput, calls=%fused_computation.2.clone.1 | convolution fusion | flops 2150891520 | bytes 9442308 | tf_op jit(solution)/shard_map/while/body/eval_jaxpr/sba,sbc->sac/dot_general | solution.py:45
  16.2 4.1 %collective-permute-start.1 = (f32[2,512,512]{1,2,0:T(8,128)S(1)}, f32[2,512,512]{1,2,0:T(8,128)}, u32[]{:S(2)}, u32[]{:S(2)}) collective-permute-start(f32[2,512,512]{1,2,0:T(8,128)S(1)} %slice.75), channel_id=1, source_target_pairs={{0,1},{1,2},{2,3},{3,4},{4,5},{5,6},{6,7},{7,8},{8,9},{9,10},{10,1... | collective-permute-start | bytes 6291464 | tf_op jit(solution)/shard_map/while/body/eval_jaxpr/ppermute | solution.py:10
  22.6 3.5 collective-permute-start
  27.5 42.5 %collective-permute-done = f32[512,512]{0,1:T(8,128)} collective-permute-done((f32[512,512]{0,1:T(8,128)}, f32[512,512]{0,1:T(8,128)}, u32[]{:S(2)}, u32[]{:S(2)}) %collective-permute-start) | collective-permute-done | bytes 1048608 | tf_op jit(solution)/shard_map/while/body/eval_jaxpr/ppermute | solution.py:10
  72.5 2.9 collective-permute-start.2
  76.4 6.1 %collective-permute-done.2 = bf16[512,512]{0,1:T(8,128)(2,1)} collective-permute-done((bf16[512,512]{0,1:T(8,128)(2,1)S(1)}, bf16[512,512]{0,1:T(8,128)(2,1)}, u32[]{:S(2)}, u32[]{:S(2)}) %collective-permute-start.2) | collective-permute-done | bytes 524320 | tf_op jit(solution)/shard_map/while/body/eval_jaxpr/ppermute | solution.py:10
  83.8 6.8 %multiply_bitcast_fusion.2 = f32[4,512,512]{1,2,0:T(8,128)} fusion(bf16[4,512,512]{2,1,0:T(8,128)(2,1)} %get-tuple-element.390, f32[4]{0:T(128)S(1)} %get-tuple-element.391, bf16[2,4,512,512]{3,2,1,0:T(8,128)(2,1)} %get-tuple-element.387, s32[]{:T(128)S(6)} %min.21, bf16[512,512]{0,1:T(8,128)(2,1)} %get-tuple-element.370, ...), kind=kOutput, calls=%fused_computation.2.clone.1 | convolution fusion | flops 2150891520 | bytes 9442308 | tf_op jit(solution)/shard_map/while/body/eval_jaxpr/sba,sbc->sac/dot_general | solution.py:45
  99.8 42.7 %collective-permute-done = f32[512,512]{0,1:T(8,128)} collective-permute-done((f32[512,512]{0,1:T(8,128)}, f32[512,512]{0,1:T(8,128)}, u32[]{:S(2)}, u32[]{:S(2)}) %collective-permute-start) | collective-permute-done | bytes 1048608 | tf_op jit(solution)/shard_map/while/body/eval_jaxpr/ppermute | solution.py:10
  145.1 2.9 collective-permute-start.2
  149.1 6.1 %collective-permute-done.2 = bf16[512,512]{0,1:T(8,128)(2,1)} collective-permute-done((bf16[512,512]{0,1:T(8,128)(2,1)S(1)}, bf16[512,512]{0,1:T(8,128)(2,1)}, u32[]{:S(2)}, u32[]{:S(2)}) %collective-permute-start.2) | collective-permute-done | bytes 524320 | tf_op jit(solution)/shard_map/while/body/eval_jaxpr/ppermute | solution.py:10
  156.5 6.8 %multiply_bitcast_fusion.2 = f32[4,512,512]{1,2,0:T(8,128)} fusion(bf16[4,512,512]{2,1,0:T(8,128)(2,1)} %get-tuple-element.390, f32[4]{0:T(128)S(1)} %get-tuple-element.391, bf16[2,4,512,512]{3,2,1,0:T(8,128)(2,1)} %get-tuple-element.387, s32[]{:T(128)S(6)} %min.21, bf16[512,512]{0,1:T(8,128)(2,1)} %get-tuple-element.370, ...), kind=kOutput, calls=%fused_computation.2.clone.1 | convolution fusion | flops 2150891520 | bytes 9442308 | tf_op jit(solution)/shard_map/while/body/eval_jaxpr/sba,sbc->sac/dot_general | solution.py:45
  172.5 41.5 %collective-permute-done = f32[512,512]{0,1:T(8,128)} collective-permute-done((f32[512,512]{0,1:T(8,128)}, f32[512,512]{0,1:T(8,128)}, u32[]{:S(2)}, u32[]{:S(2)}) %collective-permute-start) | collective-permute-done | bytes 1048608 | tf_op jit(solution)/shard_map/while/body/eval_jaxpr/ppermute | solution.py:10
  216.5 2.9 collective-permute-start.2
  220.5 6.1 %collective-permute-done.2 = bf16[512,512]{0,1:T(8,128)(2,1)} collective-permute-done((bf16[512,512]{0,1:T(8,128)(2,1)S(1)}, bf16[512,512]{0,1:T(8,128)(2,1)}, u32[]{:S(2)}, u32[]{:S(2)}) %collective-permute-start.2) | collective-permute-done | bytes 524320 | tf_op jit(solution)/shard_map/while/body/eval_jaxpr/ppermute | solution.py:10
  227.8 6.8 %multiply_bitcast_fusion.2 = f32[4,512,512]{1,2,0:T(8,128)} fusion(bf16[4,512,512]{2,1,0:T(8,128)(2,1)} %get-tuple-element.390, f32[4]{0:T(128)S(1)} %get-tuple-element.391, bf16[2,4,512,512]{3,2,1,0:T(8,128)(2,1)} %get-tuple-element.387, s32[]{:T(128)S(6)} %min.21, bf16[512,512]{0,1:T(8,128)(2,1)} %get-tuple-element.370, ...), kind=kOutput, calls=%fused_computation.2.clone.1 | convolution fusion | flops 2150891520 | bytes 9442308 | tf_op jit(solution)/shard_map/while/body/eval_jaxpr/sba,sbc->sac/dot_general | solution.py:45
  240.7 2.6 collective-permute-start
  244.6 40.7 %collective-permute-done = f32[512,512]{0,1:T(8,128)} collective-permute-done((f32[512,512]{0,1:T(8,128)}, f32[512,512]{0,1:T(8,128)}, u32[]{:S(2)}, u32[]{:S(2)}) %collective-permute-start) | collective-permute-done | bytes 1048608 | tf_op jit(solution)/shard_map/while/body/eval_jaxpr/ppermute | solution.py:10
  287.9 2.9 collective-permute-start.2
  291.9 6.1 %collective-permute-done.2 = bf16[512,512]{0,1:T(8,128)(2,1)} collective-permute-done((bf16[512,512]{0,1:T(8,128)(2,1)S(1)}, bf16[512,512]{0,1:T(8,128)(2,1)}, u32[]{:S(2)}, u32[]{:S(2)}) %collective-permute-start.2) | collective-permute-done | bytes 524320 | tf_op jit(solution)/shard_map/while/body/eval_jaxpr/ppermute | solution.py:10
  299.2 6.8 %multiply_bitcast_fusion.2 = f32[4,512,512]{1,2,0:T(8,128)} fusion(bf16[4,512,512]{2,1,0:T(8,128)(2,1)} %get-tuple-element.390, f32[4]{0:T(128)S(1)} %get-tuple-element.391, bf16[2,4,512,512]{3,2,1,0:T(8,128)(2,1)} %get-tuple-element.387, s32[]{:T(128)S(6)} %min.21, bf16[512,512]{0,1:T(8,128)(2,1)} %get-tuple-element.370, ...), kind=kOutput, calls=%fused_computation.2.clone.1 | convolution fusion | flops 2150891520 | bytes 9442308 | tf_op jit(solution)/shard_map/while/body/eval_jaxpr/sba,sbc->sac/dot_general | solution.py:45
  316.0 41.7 %collective-permute-done = f32[512,512]{0,1:T(8,128)} collective-permute-done((f32[512,512]{0,1:T(8,128)}, f32[512,512]{0,1:T(8,128)}, u32[]{:S(2)}, u32[]{:S(2)}) %collective-permute-start) | collective-permute-done | bytes 1048608 | tf_op jit(solution)/shard_map/while/body/eval_jaxpr/ppermute | solution.py:10
  360.2 2.9 collective-permute-start.2
  364.2 6.1 %collective-permute-done.2 = bf16[512,512]{0,1:T(8,128)(2,1)} collective-permute-done((bf16[512,512]{0,1:T(8,128)(2,1)S(1)}, bf16[512,512]{0,1:T(8,128)(2,1)}, u32[]{:S(2)}, u32[]{:S(2)}) %collective-permute-start.2) | collective-permute-done | bytes 524320 | tf_op jit(solution)/shard_map/while/body/eval_jaxpr/ppermute | solution.py:10
  (64 shorter events, 71.5 us)
Async XLA Ops:
  16.2 53.7 %collective-permute-start.1 = (f32[2,512,512]{1,2,0:T(8,128)S(1)}, f32[2,512,512]{1,2,0:T(8,128)}, u32[]{:S(2)}, u32[]{:S(2)}) collective-permute-start(f32[2,512,512]{1,2,0:T(8,128)S(1)} %slice.75), channel_id=1, source_target_pairs={{0,1},{1,2},{2,3},{3,4},{4,5},{5,6},{6,7},{7,8},{8,9},{9,10},{10,1... | collective-permute-start | bytes 6291464 | tf_op jit(solution)/shard_map/while/body/eval_jaxpr/ppermute | solution.py:10
  22.6 47.3 %collective-permute-start = (f32[512,512]{0,1:T(8,128)}, f32[512,512]{0,1:T(8,128)}, u32[]{:S(2)}, u32[]{:S(2)}) collective-permute-start(f32[512,512]{0,1:T(8,128)} %slice_bitcast_fusion.2), channel_id=1, source_target_pairs={{0,2},{1,3},{2,4},{3,5},{4,6},{5,7},{6,8},{7,9},{8,10},{9,11},{10,... | collective-permute-start | bytes 3145736 | tf_op jit(solution)/shard_map/while/body/eval_jaxpr/ppermute | solution.py:10
  72.5 10.0 %collective-permute-start.2 = (bf16[512,512]{0,1:T(8,128)(2,1)S(1)}, bf16[512,512]{0,1:T(8,128)(2,1)}, u32[]{:S(2)}, u32[]{:S(2)}) collective-permute-start(bf16[512,512]{0,1:T(8,128)(2,1)S(1)} %get-tuple-element.353), channel_id=1, source_target_pairs={{0,64},{64,128},{128,192},{1,65},{65,129},{129,193},{2,66},{66,130... | collective-permute-start | bytes 1572872 | tf_op jit(solution)/shard_map/while/body/eval_jaxpr/ppermute | solution.py:10
  92.4 50.2 %collective-permute-start.1 = (f32[2,512,512]{1,2,0:T(8,128)S(1)}, f32[2,512,512]{1,2,0:T(8,128)}, u32[]{:S(2)}, u32[]{:S(2)}) collective-permute-start(f32[2,512,512]{1,2,0:T(8,128)S(1)} %slice.75), channel_id=1, source_target_pairs={{0,1},{1,2},{2,3},{3,4},{4,5},{5,6},{6,7},{7,8},{8,9},{9,10},{10,1... | collective-permute-start | bytes 6291464 | tf_op jit(solution)/shard_map/while/body/eval_jaxpr/ppermute | solution.py:10
  96.6 46.0 %collective-permute-start = (f32[512,512]{0,1:T(8,128)}, f32[512,512]{0,1:T(8,128)}, u32[]{:S(2)}, u32[]{:S(2)}) collective-permute-start(f32[512,512]{0,1:T(8,128)} %slice_bitcast_fusion.2), channel_id=1, source_target_pairs={{0,2},{1,3},{2,4},{3,5},{4,6},{5,7},{6,8},{7,9},{8,10},{9,11},{10,... | collective-permute-start | bytes 3145736 | tf_op jit(solution)/shard_map/while/body/eval_jaxpr/ppermute | solution.py:10
  145.1 10.0 %collective-permute-start.2 = (bf16[512,512]{0,1:T(8,128)(2,1)S(1)}, bf16[512,512]{0,1:T(8,128)(2,1)}, u32[]{:S(2)}, u32[]{:S(2)}) collective-permute-start(bf16[512,512]{0,1:T(8,128)(2,1)S(1)} %get-tuple-element.353), channel_id=1, source_target_pairs={{0,64},{64,128},{128,192},{1,65},{65,129},{129,193},{2,66},{66,130... | collective-permute-start | bytes 1572872 | tf_op jit(solution)/shard_map/while/body/eval_jaxpr/ppermute | solution.py:10
  165.1 48.9 %collective-permute-start.1 = (f32[2,512,512]{1,2,0:T(8,128)S(1)}, f32[2,512,512]{1,2,0:T(8,128)}, u32[]{:S(2)}, u32[]{:S(2)}) collective-permute-start(f32[2,512,512]{1,2,0:T(8,128)S(1)} %slice.75), channel_id=1, source_target_pairs={{0,1},{1,2},{2,3},{3,4},{4,5},{5,6},{6,7},{7,8},{8,9},{9,10},{10,1... | collective-permute-start | bytes 6291464 | tf_op jit(solution)/shard_map/while/body/eval_jaxpr/ppermute | solution.py:10
  169.3 44.7 %collective-permute-start = (f32[512,512]{0,1:T(8,128)}, f32[512,512]{0,1:T(8,128)}, u32[]{:S(2)}, u32[]{:S(2)}) collective-permute-start(f32[512,512]{0,1:T(8,128)} %slice_bitcast_fusion.2), channel_id=1, source_target_pairs={{0,2},{1,3},{2,4},{3,5},{4,6},{5,7},{6,8},{7,9},{8,10},{9,11},{10,... | collective-permute-start | bytes 3145736 | tf_op jit(solution)/shard_map/while/body/eval_jaxpr/ppermute | solution.py:10
  216.5 10.0 %collective-permute-start.2 = (bf16[512,512]{0,1:T(8,128)(2,1)S(1)}, bf16[512,512]{0,1:T(8,128)(2,1)}, u32[]{:S(2)}, u32[]{:S(2)}) collective-permute-start(bf16[512,512]{0,1:T(8,128)(2,1)S(1)} %get-tuple-element.353), channel_id=1, source_target_pairs={{0,64},{64,128},{128,192},{1,65},{65,129},{129,193},{2,66},{66,130... | collective-permute-start | bytes 1572872 | tf_op jit(solution)/shard_map/while/body/eval_jaxpr/ppermute | solution.py:10
  236.4 48.9 %collective-permute-start.1 = (f32[2,512,512]{1,2,0:T(8,128)S(1)}, f32[2,512,512]{1,2,0:T(8,128)}, u32[]{:S(2)}, u32[]{:S(2)}) collective-permute-start(f32[2,512,512]{1,2,0:T(8,128)S(1)} %slice.75), channel_id=1, source_target_pairs={{0,1},{1,2},{2,3},{3,4},{4,5},{5,6},{6,7},{7,8},{8,9},{9,10},{10,1... | collective-permute-start | bytes 6291464 | tf_op jit(solution)/shard_map/while/body/eval_jaxpr/ppermute | solution.py:10
  240.7 44.7 %collective-permute-start = (f32[512,512]{0,1:T(8,128)}, f32[512,512]{0,1:T(8,128)}, u32[]{:S(2)}, u32[]{:S(2)}) collective-permute-start(f32[512,512]{0,1:T(8,128)} %slice_bitcast_fusion.2), channel_id=1, source_target_pairs={{0,2},{1,3},{2,4},{3,5},{4,6},{5,7},{6,8},{7,9},{8,10},{9,11},{10,... | collective-permute-start | bytes 3145736 | tf_op jit(solution)/shard_map/while/body/eval_jaxpr/ppermute | solution.py:10
  287.9 10.0 %collective-permute-start.2 = (bf16[512,512]{0,1:T(8,128)(2,1)S(1)}, bf16[512,512]{0,1:T(8,128)(2,1)}, u32[]{:S(2)}, u32[]{:S(2)}) collective-permute-start(bf16[512,512]{0,1:T(8,128)(2,1)S(1)} %get-tuple-element.353), channel_id=1, source_target_pairs={{0,64},{64,128},{128,192},{1,65},{65,129},{129,193},{2,66},{66,130... | collective-permute-start | bytes 1572872 | tf_op jit(solution)/shard_map/while/body/eval_jaxpr/ppermute | solution.py:10
  307.8 49.8 %collective-permute-start.1 = (f32[2,512,512]{1,2,0:T(8,128)S(1)}, f32[2,512,512]{1,2,0:T(8,128)}, u32[]{:S(2)}, u32[]{:S(2)}) collective-permute-start(f32[2,512,512]{1,2,0:T(8,128)S(1)} %slice.75), channel_id=1, source_target_pairs={{0,1},{1,2},{2,3},{3,4},{4,5},{5,6},{6,7},{7,8},{8,9},{9,10},{10,1... | collective-permute-start | bytes 6291464 | tf_op jit(solution)/shard_map/while/body/eval_jaxpr/ppermute | solution.py:10
  312.0 45.6 %collective-permute-start = (f32[512,512]{0,1:T(8,128)}, f32[512,512]{0,1:T(8,128)}, u32[]{:S(2)}, u32[]{:S(2)}) collective-permute-start(f32[512,512]{0,1:T(8,128)} %slice_bitcast_fusion.2), channel_id=1, source_target_pairs={{0,2},{1,3},{2,4},{3,5},{4,6},{5,7},{6,8},{7,9},{8,10},{9,11},{10,... | collective-permute-start | bytes 3145736 | tf_op jit(solution)/shard_map/while/body/eval_jaxpr/ppermute | solution.py:10
  360.2 10.0 %collective-permute-start.2 = (bf16[512,512]{0,1:T(8,128)(2,1)S(1)}, bf16[512,512]{0,1:T(8,128)(2,1)}, u32[]{:S(2)}, u32[]{:S(2)}) collective-permute-start(bf16[512,512]{0,1:T(8,128)(2,1)S(1)} %get-tuple-element.353), channel_id=1, source_target_pairs={{0,64},{64,128},{128,192},{1,65},{65,129},{129,193},{2,66},{66,130... | collective-permute-start | bytes 1572872 | tf_op jit(solution)/shard_map/while/body/eval_jaxpr/ppermute | solution.py:10
where the time goes:
time: 372 us; the launch traced here: 370 us
  waiting for transfers between devices  239 us (64%)
  local copies, waits for them, and re-layouts  42.9 us (12%)
  starting transfers between devices  39 us (10%)
  matrix products  34.1 us (9%)
  other arithmetic  14.5 us (4%)
    ppermute x15, waiting for transfers between devices, shifted(): return lax.ppermute(array, axis, pairs)  239 us
    ppermute x15, starting transfers between devices, shifted(): return lax.ppermute(array, axis, pairs)  39 us
    dot_general x5, matrix products, advance(): jnp.einsum('sba,sbc->sac', bra_here, moved, preferred_element_type=jnp.fl...  34.1 us
    select_n x5, other arithmetic, advance(): result = jnp.where(valid, updated, result)  12.6 us
    select_n x20, local copies, waits for them, and re-layouts, advance(): result = jnp.where(valid, updated, result)  11.7 us
    squeeze x5, local copies, waits for them, and re-layouts, advance(): double = shifted(parts[3], 'sector', 2)  11.5 us
    slice x5, local copies, waits for them, and re-layouts, advance(): arrived = shifted(parts[1:3], 'sector', 1)  8.81 us
  transfers between devices with their start and end apart: 15, of which 10 were waited for; matrix products, arithmetic and copies ran while one was open for 6% of the time, Pallas kernels for 0%

commit v1 on v0

v1 whole, which is shorter than its diff:
```python
import jax
import jax.numpy as jnp
from jax import lax
from jax.experimental import pallas as pl
from jax.experimental.pallas import tpu as pltpu
from jax.sharding import PartitionSpec as P

MESH = pl.DeviceIdType.MESH
WIDE = 128
ROWS = 64
F32 = jnp.float32
BF16 = jnp.bfloat16


def chain_kernel(
    dims, flags, env, bra, ket, out,
    env_v, bra_v, ket_v, stay, three, s_out, s_in, x_out, x_in, e_out,
    env_sem, bra_sem, ket_sem, s_send, s_recv, x_send, x_recv, y_send, y_recv, o_sem,
):
    site, sector = lax.axis_index("site"), lax.axis_index("sector")
    sites, sectors = lax.axis_size("site"), lax.axis_size("sector")
    core = lax.rem(sector, 2)
    pairs, size = env_v.shape[0], env_v.shape[1]
    wides, chunks = size // WIDE, size // ROWS
    other = sector + 1 - 2 * core
    ahead = lax.rem(sector + 2, sectors)
    behind = lax.rem(sector + sectors - 2, sectors)
    first, last = site == 0, site == sites - 1

    def env_load(p):
        return pltpu.make_async_copy(env.at[p, 0], env_v.at[p], env_sem.at[p])

    def bra_load():
        return pltpu.make_async_copy(bra.at[0, :, 0], bra_v, bra_sem)

    def ket_load(p):
        return pltpu.make_async_copy(ket.at[0, p, :, 0], ket_v.at[p], ket_sem.at[p])

    def send_s(p, i):
        rows = pl.ds(pl.multiple_of(i * WIDE, WIDE), WIDE)
        return pltpu.make_async_remote_copy(
            s_out.at[p, rows], s_in.at[p, rows], s_send.at[p, i], s_recv.at[p, i],
            device_id=(site, other), device_id_type=MESH)

    def send_x(p, r):
        rows = pl.ds(pl.multiple_of(r * ROWS, ROWS), ROWS)
        return pltpu.make_async_remote_copy(
            x_out.at[p, rows], x_in.at[p, rows], x_send.at[p, r], x_recv.at[p, r],
            device_id=(site, ahead), device_id_type=MESH)

    def send_y(p, r):
        rows = pl.ds(pl.multiple_of(r * ROWS, ROWS), ROWS)
        return pltpu.make_async_remote_copy(
            e_out.at[p, rows], env_v.at[p, rows], y_send.at[p, r], y_recv.at[p, r],
            device_id=(lax.rem(site + 1, sites), sector), device_id_type=MESH)

    def store(p, r):
        rows = pl.ds(pl.multiple_of(r * ROWS, ROWS), ROWS)
        return pltpu.make_async_copy(e_out.at[p, rows], out.at[0, p, 0, rows], o_sem.at[p, r])

    barrier = pltpu.get_barrier_semaphore()
    for partner in (other, ahead, behind):
        pl.semaphore_signal(barrier, inc=1, device_id=(site, partner), device_id_type=MESH)
    for partner in (lax.rem(site + 1, sites), lax.rem(site + sites - 1, sites)):
        pl.semaphore_signal(barrier, inc=1, device_id=(partner, sector), device_id_type=MESH)

    @pl.when(first)
    def _():
        env_load(0).start()

    bra_load().start()
    ket_load(0).start()

    @pl.when(first)
    def _():
        env_load(1).start()

    ket_load(1).start()

    pl.semaphore_wait(barrier, 5)
    bra_load().wait()
    dim_first, dim_next = dims[0, sector], dims[site + 1, sector]
    on = [flags[0, s, 0].astype(F32) for s in range(4)]
    has_before = (sector >= 2).astype(jnp.int32)
    lane = lax.broadcasted_iota(jnp.int32, (ROWS, size), 1)
    row = lax.broadcasted_iota(jnp.int32, (ROWS, size), 0)

    def dot(a, b):
        return jnp.dot(a, b, preferred_element_type=F32)

    def x_of(p, i):
        send_s(p, i).wait_recv()
        rows = pl.ds(pl.multiple_of(i * WIDE, WIDE), WIDE)
        x_out[p, rows] = (three[rows] + s_in[p, rows].astype(F32)).astype(BF16)
        for k in range(WIDE // ROWS):
            send_x(p, i * (WIDE // ROWS) + k).start()

    def compute(p):
        ket_load(p).wait()

        @pl.when(first)
        def _():
            env_load(p).wait()

            def mask(r, carry):
                rows = pl.ds(pl.multiple_of(r * ROWS, ROWS), ROWS)
                inside = jnp.logical_and(row + r * ROWS < dim_first, lane < dim_first)
                env_v[p, rows] = jnp.where(inside, env_v[p, rows].astype(F32), 0.0).astype(BF16)
                return carry

            lax.fori_loop(0, chunks, mask, 0)

        @pl.when(jnp.logical_not(first))
        def _():
            def arrive(r, carry):
                send_y(p, r).wait_recv()
                return carry

            lax.fori_loop(0, chunks, arrive, 0)

        def step(i, carry):
            rows = pl.ds(pl.multiple_of(i * WIDE, WIDE), WIDE)
            here = env_v[p]
            left = [
                (lax.dot_general(bra_v[s, :, rows], here, (((0,), (0,)), ((), ())),
                                 preferred_element_type=F32) * on[s]).astype(BF16)
                for s in range(4)
            ]
            s_out[p, rows] = (dot(left[1], ket_v[p, 1]) + dot(left[2], ket_v[p, 2])).astype(BF16)
            send_s(p, i).start()
            double = dot(left[3], ket_v[p, 3])

            @pl.when(core == 1)
            def _():
                x_out[p, rows] = double.astype(BF16)
                for k in range(WIDE // ROWS):
                    send_x(p, i * (WIDE // ROWS) + k).start()

            @pl.when(core == 0)
            def _():
                three[rows] = double

            stay[p, rows] = dot(left[0], ket_v[p, 0])

            @pl.when(jnp.logical_and(core == 0, i > 0))
            def _():
                x_of(p, i - 1)

            return carry

        lax.fori_loop(0, wides, step, 0)

        @pl.when(core == 0)
        def _():
            x_of(p, wides - 1)

        @pl.when(core == 1)
        def _():
            def arrive(i, carry):
                send_s(p, i).wait_recv()
                rows = pl.ds(pl.multiple_of(i * WIDE, WIDE), WIDE)
                stay[p, rows] += s_in[p, rows].astype(F32)
                return carry

            lax.fori_loop(0, wides, arrive, 0)

    def finish(p):
        def step(r, carry):
            rows = pl.ds(pl.multiple_of(r * ROWS, ROWS), ROWS)
            send_x(p, r).wait_recv()
            arrived = jnp.where(has_before > 0, x_in[p, rows].astype(F32), 0.0)
            inside = jnp.logical_and(row + r * ROWS < dim_next, lane < dim_next)
            e_out[p, rows] = jnp.where(inside, stay[p, rows] + arrived, 0.0).astype(BF16)

            @pl.when(jnp.logical_not(last))
            def _():
                send_y(p, r).start()

            store(p, r).start()
            return carry

        lax.fori_loop(0, chunks, step, 0)

    def stage(t, carry):
        finishing = jnp.where(first, t // 2, lax.rem(t, 2))
        p = jnp.where(first, lax.rem(t, 2), t // 2)

        @pl.when(finishing == 0)
        def _():
            compute(p)

        @pl.when(finishing == 1)
        def _():
            finish(p)

        return carry

    lax.fori_loop(0, 2 * pairs, stage, 0)

    def drain(t, carry):
        p, r = t // chunks, lax.rem(t, chunks)
        send_x(p, r).wait_send()
        store(p, r).wait()

        @pl.when(jnp.logical_not(last))
        def _():
            send_y(p, r).wait_send()

        return carry

    lax.fori_loop(0, pairs * chunks, drain, 0)

    def drain_s(t, carry):
        send_s(t // wides, lax.rem(t, wides)).wait_send()
        return carry

    lax.fori_loop(0, pairs * wides, drain_s, 0)


def per_device(env_in, bra, ket, sector_dims, flags):
    pairs, size = env_in.shape[0], env_in.shape[-1]
    wides, chunks = size // WIDE, size // ROWS
    blocks = (pairs, size, size)
    dma = pltpu.SemaphoreType.DMA
    smem = pl.BlockSpec(memory_space=pltpu.SMEM)
    hbm = pl.BlockSpec(memory_space=pl.ANY)
    return pl.pallas_call(
        chain_kernel,
        out_shape=jax.ShapeDtypeStruct((1, pairs, 1, size, size), BF16),
        in_specs=[smem, smem, hbm, hbm, hbm],
        out_specs=hbm,
        scratch_shapes=[
            pltpu.VMEM(blocks, BF16),
            pltpu.VMEM((4, size, size), BF16),
            pltpu.VMEM((pairs, 4, size, size), BF16),
            pltpu.VMEM(blocks, F32),
            pltpu.VMEM((size, size), F32),
            pltpu.VMEM(blocks, BF16),
            pltpu.VMEM(blocks, BF16),
            pltpu.VMEM(blocks, BF16),
            pltpu.VMEM(blocks, BF16),
            pltpu.VMEM(blocks, BF16),
            dma((pairs,)),
            dma,
            dma((pairs,)),
            dma((pairs, wides)),
            dma((pairs, wides)),
            dma((pairs, chunks)),
            dma((pairs, chunks)),
            dma((pairs, chunks)),
            dma((pairs, chunks)),
            dma((pairs, chunks)),
        ],
        compiler_params=pltpu.CompilerParams(
            collective_id=0, has_side_effects=True, vmem_limit_bytes=56 << 20
        ),
        cost_estimate=pl.CostEstimate(
            flops=pairs * 16 * size**3, bytes_accessed=16 * size * size * 2, transcendentals=0
        ),
    )(sector_dims, flags, env_in, bra, ket)


def solution(mesh):
    in_specs = (
        P(None, "sector", None, None),
        P("site", None, "sector", None, None),
        P("site", None, None, "sector", None, None),
        P(),
        P("site", None, "sector"),
    )
    out_specs = P("site", None, "sector", None, None)
    return jax.shard_map(
        per_device, mesh=mesh, in_specs=in_specs, out_specs=out_specs, check_vma=False
    )
```

time: 372 us -> 102 us (0.27)
  the two profiles are of different devices: /device:TPU:23 before, /device:TPU:24 now
where the time goes in v1:
time: 102 us
  Pallas kernels  98.5 us (97%)
  local copies, waits for them, and re-layouts  3.57 us (4%)
    pallas_call x1, Pallas kernels, per_device(): pl.pallas_call(chain_kernel, out_shape=jax.ShapeDtypeStruct((1, pairs, 1,...  98.5 us
    unnamed x2, local copies, waits for them, and re-layouts  3.57 us

profile of v1, /device:TPU:24, one launch (start us, length us, event | category | flops | bytes accessed | tf_op | source)
XLA Modules:
  0.0 102.1 jit_solution(2776407241667547956)
XLA Ops:
  0.0 1.3 %copy.6.flags = s32[1,4,1]{2,1,0:T(4,128)} copy(s32[1,4,1]{1,2,0:T(1,128)} %param.9) | data formatting | bytes 32 | tf_op args[4]
  1.3 98.5 %shard_map.55 = bf16[1,2,1,512,512]{4,3,2,1,0:T(8,128)(2,1)} custom-call(s32[5,64]{1,0:T(8,128)} %dims.1, s32[1,4,1]{2,1,0:T(4,128)} %copy.6.flags, bf16[2,1,512,512]{3,2,1,0:T(8,128)(2,1)} %env.1, bf16[1,4,1,512,512]{4,3,2,1,0:T(8,128)(2,1)} %bra.1, bf16[1,2,4,1,512,512]{5,4,3,2,1,0:T(8,128)(2,1)} %ket.1), custom_call_target="tpu_custom_call" | custom-call | flops 4294967296 | bytes 8388608 | tf_op jit(solution)/shard_map/pallas_call | solution.py:227
  99.8 2.3 %copy.8 = bf16[1,2,1,512,512]{4,3,2,1,0:T(8,128)(2,1)} copy(bf16[1,2,1,512,512]{4,3,2,1,0:T(8,128)(2,1)} %shard_map.55) | data formatting | bytes 2097152

commit v2 on v1

v2 whole, which is shorter than its diff:
```python
import jax
import jax.numpy as jnp
from jax import lax
from jax.experimental import pallas as pl
from jax.experimental.pallas import tpu as pltpu
from jax.sharding import PartitionSpec as P

MESH = pl.DeviceIdType.MESH
WIDE = 128
ROWS = 64
TURN = 8
TURN_FIRST = 5
F32 = jnp.float32
BF16 = jnp.bfloat16


def chain_kernel(
    dims, flags, env, bra, ket, out,
    env_v, bra_v, ket_v, stay, three, s_out, s_in, x_out, x_in,
    env_sem, bra_sem, ket_sem, s_send, s_recv, x_send, x_recv, y_send, y_recv,
):
    site, sector = lax.axis_index("site"), lax.axis_index("sector")
    sites, sectors = lax.axis_size("site"), lax.axis_size("sector")
    core = lax.rem(sector, 2)
    pairs, size = env_v.shape[0], env_v.shape[1]
    wides, chunks = size // WIDE, size // ROWS
    other = sector + 1 - 2 * core
    ahead = lax.rem(sector + 2, sectors)
    behind = lax.rem(sector + sectors - 2, sectors)
    first, last = site == 0, site == sites - 1

    def env_load(p):
        return pltpu.make_async_copy(env.at[p, 0], env_v.at[p], env_sem.at[p])

    def bra_load(s):
        return pltpu.make_async_copy(bra.at[0, s, 0], bra_v.at[s], bra_sem.at[s])

    def ket_load(p, s):
        return pltpu.make_async_copy(ket.at[0, p, s, 0], ket_v.at[p, s], ket_sem.at[p, s])

    def send_s(p, i):
        rows = pl.ds(pl.multiple_of(i * WIDE, WIDE), WIDE)
        return pltpu.make_async_remote_copy(
            s_out.at[p, rows], s_in.at[p, rows], s_send.at[p, i], s_recv.at[p, i],
            device_id=(site, other), device_id_type=MESH)

    def send_x(p, r):
        rows = pl.ds(pl.multiple_of(r * ROWS, ROWS), ROWS)
        return pltpu.make_async_remote_copy(
            x_out.at[p, rows], x_in.at[p, rows], x_send.at[p, r], x_recv.at[p, r],
            device_id=(site, ahead), device_id_type=MESH)

    def send_y(p, r):
        rows = pl.ds(pl.multiple_of(r * ROWS, ROWS), ROWS)
        return pltpu.make_async_remote_copy(
            out.at[0, p, 0, rows], env_v.at[p, rows], y_send.at[p, r], y_recv.at[p, r],
            device_id=(lax.rem(site + 1, sites), sector), device_id_type=MESH)

    barrier = pltpu.get_barrier_semaphore()
    for partner in (other, ahead, behind):
        pl.semaphore_signal(barrier, inc=1, device_id=(site, partner), device_id_type=MESH)
    for partner in (lax.rem(site + 1, sites), lax.rem(site + sites - 1, sites)):
        pl.semaphore_signal(barrier, inc=1, device_id=(partner, sector), device_id_type=MESH)

    @pl.when(first)
    def _():
        env_load(0).start()

    for s in (3, 1, 2, 0):
        bra_load(s).start()
        ket_load(0, s).start()

    dim_first, dim_next = dims[0, sector], dims[site + 1, sector]
    on = [flags[0, 0, s].astype(F32) for s in range(4)]
    has_before = (sector >= 2).astype(jnp.int32)
    lane = lax.broadcasted_iota(jnp.int32, (ROWS, size), 1)
    row = lax.broadcasted_iota(jnp.int32, (ROWS, size), 0)

    def dot(a, b):
        return jnp.dot(a, b, preferred_element_type=F32)

    def x_of(p, i):
        send_s(p, i).wait_recv()
        rows = pl.ds(pl.multiple_of(i * WIDE, WIDE), WIDE)
        x_out[p, rows] = (three[rows] + s_in[p, rows].astype(F32)).astype(BF16)
        for k in range(WIDE // ROWS):
            send_x(p, i * (WIDE // ROWS) + k).start()

    def cover(p):
        @pl.when(first)
        def _():
            env_load(p).wait()

            def mask(r, carry):
                rows = pl.ds(pl.multiple_of(r * ROWS, ROWS), ROWS)
                inside = jnp.logical_and(row + r * ROWS < dim_first, lane < dim_first)
                env_v[p, rows] = jnp.where(inside, env_v[p, rows].astype(F32), 0.0).astype(BF16)
                return carry

            lax.fori_loop(0, chunks, mask, 0)

    def enter(p):
        @pl.when(jnp.logical_not(first))
        def _():
            def arrive(r, carry):
                send_y(p, r).wait_recv()
                return carry

            lax.fori_loop(0, chunks, arrive, 0)

    def compute(p, i):
        rows = pl.ds(pl.multiple_of(i * WIDE, WIDE), WIDE)
        here = env_v[p]

        def part(s):
            @pl.when(i == 0)
            def _():
                if p == 0:
                    bra_load(s).wait()
                ket_load(p, s).wait()

            left = lax.dot_general(bra_v[s, :, rows], here, (((0,), (0,)), ((), ())),
                                   preferred_element_type=F32)
            return dot((left * on[s]).astype(BF16), ket_v[p, s])

        def single():
            s_out[p, rows] = (part(1) + part(2)).astype(BF16)
            send_s(p, i).start()

        @pl.when(core == 1)
        def _():
            x_out[p, rows] = part(3).astype(BF16)
            for k in range(WIDE // ROWS):
                send_x(p, i * (WIDE // ROWS) + k).start()
            single()
            stay[p, rows] = part(0)

        @pl.when(core == 0)
        def _():
            single()
            three[rows] = part(3)

            @pl.when(jnp.logical_not(first))
            def _():
                x_of(p, i)

            stay[p, rows] = part(0)

            @pl.when(first)
            def _():
                @pl.when(i > 0)
                def _():
                    x_of(p, i - 1)

                @pl.when(i == wides - 1)
                def _():
                    x_of(p, i)

    def finish(p, r):
        rows = pl.ds(pl.multiple_of(r * ROWS, ROWS), ROWS)

        @pl.when(core == 1)
        def _():
            @pl.when(lax.rem(r, WIDE // ROWS) == 0)
            def _():
                send_s(p, r // (WIDE // ROWS)).wait_recv()

            stay[p, rows] += s_in[p, rows].astype(F32)

        send_x(p, r).wait_recv()
        arrived = jnp.where(has_before > 0, x_in[p, rows].astype(F32), 0.0)
        inside = jnp.logical_and(row + r * ROWS < dim_next, lane < dim_next)
        out[0, p, 0, rows] = jnp.where(inside, stay[p, rows] + arrived, 0.0).astype(BF16)

        @pl.when(jnp.logical_not(last))
        def _():
            send_y(p, r).start()

    turn = jnp.where(first, TURN_FIRST, TURN)

    def work(t, carry):
        k = t - turn

        @pl.when(jnp.logical_and(k >= 0, k < wides))
        def _():
            @pl.when(k == 0)
            def _():
                cover(1)
                enter(1)

            compute(1, k)

        @pl.when(t < chunks)
        def _():
            finish(0, t)

        return carry

    def first_compute(i, carry):
        compute(0, i)
        return carry

    def last_finish(r, carry):
        finish(1, r)
        return carry

    cover(0)
    pl.semaphore_wait(barrier, 5)
    enter(0)
    lax.fori_loop(0, wides, first_compute, 0)

    @pl.when(first)
    def _():
        env_load(1).start()

    for s in (3, 1, 2, 0):
        ket_load(1, s).start()
    lax.fori_loop(0, jnp.maximum(turn + wides, chunks), work, 0)
    lax.fori_loop(0, chunks, last_finish, 0)

    def drain(t, carry):
        p, r = t // chunks, lax.rem(t, chunks)
        send_x(p, r).wait_send()

        @pl.when(jnp.logical_not(last))
        def _():
            send_y(p, r).wait_send()

        return carry

    lax.fori_loop(0, pairs * chunks, drain, 0)

    def drain_s(t, carry):
        send_s(t // wides, lax.rem(t, wides)).wait_send()
        return carry

    lax.fori_loop(0, pairs * wides, drain_s, 0)


def per_device(env_in, bra, ket, sector_dims, flags):
    pairs, size = env_in.shape[0], env_in.shape[-1]
    wides, chunks = size // WIDE, size // ROWS
    blocks = (pairs, size, size)
    dma = pltpu.SemaphoreType.DMA
    smem = pl.BlockSpec(memory_space=pltpu.SMEM)
    hbm = pl.BlockSpec(memory_space=pl.ANY)
    return pl.pallas_call(
        chain_kernel,
        out_shape=pltpu.VMEM((1, pairs, 1, size, size), BF16),
        in_specs=[smem, smem, hbm, hbm, hbm],
        out_specs=pl.BlockSpec(memory_space=pltpu.VMEM),
        scratch_shapes=[
            pltpu.VMEM(blocks, BF16),
            pltpu.VMEM((4, size, size), BF16),
            pltpu.VMEM((pairs, 4, size, size), BF16),
            pltpu.VMEM(blocks, F32),
            pltpu.VMEM((size, size), F32),
            pltpu.VMEM(blocks, BF16),
            pltpu.VMEM(blocks, BF16),
            pltpu.VMEM(blocks, BF16),
            pltpu.VMEM(blocks, BF16),
            dma((pairs,)),
            dma((4,)),
            dma((pairs, 4)),
            dma((pairs, wides)),
            dma((pairs, wides)),
            dma((pairs, chunks)),
            dma((pairs, chunks)),
            dma((pairs, chunks)),
            dma((pairs, chunks)),
        ],
        compiler_params=pltpu.CompilerParams(
            collective_id=0, has_side_effects=True, vmem_limit_bytes=56 << 20
        ),
        cost_estimate=pl.CostEstimate(
            flops=pairs * 16 * size**3, bytes_accessed=16 * size * size * 2, transcendentals=0
        ),
    )(sector_dims, jnp.swapaxes(flags, 1, 2), env_in, bra, ket)


def solution(mesh):
    in_specs = (
        P(None, "sector", None, None),
        P("site", None, "sector", None, None),
        P("site", None, None, "sector", None, None),
        P(),
        P("site", None, "sector"),
    )
    out_specs = P("site", None, "sector", None, None)
    return jax.shard_map(
        per_device, mesh=mesh, in_specs=in_specs, out_specs=out_specs, check_vma=False
    )
```

time: 102 us -> 88.8 us (0.87)
  Pallas kernels: 98.5 us -> 87.7 us
  local copies, waits for them, and re-layouts: 3.57 us -> 0.97 us
    pallas_call x1, Pallas kernels: 98.5 us -> 87.7 us  [per_device(): pl.pallas_call(chain_kernel, out_shape=pltpu.VMEM((1, pairs, 1, size, siz...]
    unnamed x2 -> x1, local copies, waits for them, and re-layouts: 3.57 us -> 0.97 us
where the time goes in v2:
time: 88.8 us; the launch traced here: 88.7 us
  Pallas kernels  87.7 us (99%)
  local copies, waits for them, and re-layouts  0.97 us (1%)
    pallas_call x1, Pallas kernels, per_device(): pl.pallas_call(chain_kernel, out_shape=pltpu.VMEM((1, pairs, 1, size, siz...  87.7 us

profile of v2, /device:TPU:24, one launch (start us, length us, event | category | flops | bytes accessed | tf_op | source)
XLA Modules:
  0.0 88.7 jit_solution(18323999595451001750)
XLA Ops:
  0.0 87.7 %shard_map.55 = bf16[1,2,1,512,512]{4,3,2,1,0:T(8,128)(2,1)S(1)} custom-call(s32[5,64]{1,0:T(8,128)} %dims.1, s32[1,1,4]{2,1,0:T(1,128)} %bitcast.1, bf16[2,1,512,512]{3,2,1,0:T(8,128)(2,1)} %env.1, bf16[1,4,1,512,512]{4,3,2,1,0:T(8,128)(2,1)} %bra.1, bf16[1,2,4,1,512,512]{5,4,3,2,1,0:T(8,128)(2,1)} %ket.1), custom_call_target="tpu_custom_call" | custom-call | flops 4294967296 | bytes 8388608 | tf_op jit(solution)/shard_map/pallas_call | solution.py:247
  87.7 1.0 %copy.7 = bf16[1,2,1,512,512]{4,3,2,1,0:T(8,128)(2,1)} copy(bf16[1,2,1,512,512]{4,3,2,1,0:T(8,128)(2,1)S(1)} %shard_map.55) | data formatting | bytes 2097152

commit v3 on v2

--- a/solution.py
+++ b/solution.py
@@ -9,14 +9,16 @@
 WIDE = 128
 ROWS = 64
 TURN = 8
-TURN_FIRST = 5
+TURN_ZERO = 8
+TURN_ONE = 8
+LATE = 5
 F32 = jnp.float32
 BF16 = jnp.bfloat16
 
 
 def chain_kernel(
     dims, flags, env, bra, ket, out,
-    env_v, bra_v, ket_v, stay, three, s_out, s_in, x_out, x_in,
+    env_v, bra_v, ket_v, moved, stay, three, s_out, s_in, x_out, x_in,
     env_sem, bra_sem, ket_sem, s_send, s_recv, x_send, x_recv, y_send, y_recv,
 ):
     site, sector = lax.axis_index("site"), lax.axis_index("sector")
@@ -99,20 +101,72 @@
 
             lax.fori_loop(0, chunks, mask, 0)
 
-    def enter(p):
-        @pl.when(jnp.logical_not(first))
-        def _():
-            def arrive(r, carry):
-                send_y(p, r).wait_recv()
-                return carry
-
-            lax.fori_loop(0, chunks, arrive, 0)
-
-    def compute(p, i):
+    def arrive(p, i):
+        for k in range(WIDE // ROWS):
+            send_y(p, i * (WIDE // ROWS) + k).wait_recv()
+
+    def move(p, s, i):
+        rows = pl.ds(pl.multiple_of(i * WIDE, WIDE), WIDE)
+        moved[s, rows] = (dot(env_v[p, rows], ket_v[p, s]) * on[s]).astype(BF16)
+
+    def early(p, i):
+        arrive(p, i)
+        for s in range(4):
+            move(p, s, i)
+
+    def rest(p, s):
+        move(p, s, wides - 1)
+
+    def part(s, rows):
+        return lax.dot_general(bra_v[s, :, rows], moved[s], (((0,), (0,)), ((), ())),
+                               preferred_element_type=F32)
+
+    def by_chunk(body):
+        def step(i, carry):
+            body(i, pl.ds(pl.multiple_of(i * WIDE, WIDE), WIDE))
+            return carry
+
+        lax.fori_loop(0, wides, step, 0)
+
+    def single(p):
+        def body(i, rows):
+            s_out[p, rows] = (part(1, rows) + part(2, rows)).astype(BF16)
+            send_s(p, i).start()
+
+        by_chunk(body)
+
+    def double(p):
+        rest(p, 3)
+
+        def body(i, rows):
+            both = part(3, rows)
+
+            @pl.when(core == 1)
+            def _():
+                x_out[p, rows] = both.astype(BF16)
+                for k in range(WIDE // ROWS):
+                    send_x(p, i * (WIDE // ROWS) + k).start()
+
+            @pl.when(core == 0)
+            def _():
+                three[rows] = both
+                x_of(p, i)
+
+        by_chunk(body)
+
+    def none(p):
+        rest(p, 0)
+
+        def body(i, rows):
+            stay[p, rows] = part(0, rows)
+
+        by_chunk(body)
+
+    def compute_first(p, i):
         rows = pl.ds(pl.multiple_of(i * WIDE, WIDE), WIDE)
         here = env_v[p]
 
-        def part(s):
+        def whole(s):
             @pl.when(i == 0)
             def _():
                 if p == 0:
@@ -123,70 +177,88 @@
                                    preferred_element_type=F32)
             return dot((left * on[s]).astype(BF16), ket_v[p, s])
 
-        def single():
-            s_out[p, rows] = (part(1) + part(2)).astype(BF16)
-            send_s(p, i).start()
+        both = whole(3)
 
         @pl.when(core == 1)
         def _():
-            x_out[p, rows] = part(3).astype(BF16)
+            x_out[p, rows] = both.astype(BF16)
             for k in range(WIDE // ROWS):
                 send_x(p, i * (WIDE // ROWS) + k).start()
-            single()
-            stay[p, rows] = part(0)
 
         @pl.when(core == 0)
         def _():
-            single()
-            three[rows] = part(3)
-
-            @pl.when(jnp.logical_not(first))
-            def _():
-                x_of(p, i)
-
-            stay[p, rows] = part(0)
-
-            @pl.when(first)
-            def _():
-                @pl.when(i > 0)
-                def _():
-                    x_of(p, i - 1)
-
-                @pl.when(i == wides - 1)
-                def _():
-                    x_of(p, i)
+            three[rows] = both
+
+        s_out[p, rows] = (whole(1) + whole(2)).astype(BF16)
+        send_s(p, i).start()
+        stay[p, rows] = whole(0)
+
+        @pl.when(jnp.logical_and(core == 0, i > 0))
+        def _():
+            x_of(p, i - 1)
+
+        @pl.when(jnp.logical_and(core == 0, i == wides - 1))
+        def _():
+            x_of(p, i)
+
+    def compute_later(p, k):
+        @pl.when(k == 0)
+        def _():
+            arrive(p, wides - 1)
+
+        @pl.when(jnp.where(core == 1, k == 0, k == 2))
+        def _():
+            double(p)
+
+        @pl.when(jnp.where(core == 1, k == 1, k == 0))
+        def _():
+            rest(p, 1)
+            rest(p, 2)
+
+        @pl.when(jnp.where(core == 1, k == 2, k == 1))
+        def _():
+            single(p)
+
+        @pl.when(k == 3)
+        def _():
+            none(p)
+
+    def compute(p, k):
+        @pl.when(first)
+        def _():
+            compute_first(p, k)
+
+        @pl.when(jnp.logical_not(first))
+        def _():
+            compute_later(p, k)
 
     def finish(p, r):
         rows = pl.ds(pl.multiple_of(r * ROWS, ROWS), ROWS)
 
-        @pl.when(core == 1)
-        def _():
-            @pl.when(lax.rem(r, WIDE // ROWS) == 0)
-            def _():
-                send_s(p, r // (WIDE // ROWS)).wait_recv()
-
-            stay[p, rows] += s_in[p, rows].astype(F32)
+        @pl.when(jnp.logical_and(core == 1, lax.rem(r, WIDE // ROWS) == 0))
+        def _():
+            send_s(p, r // (WIDE // ROWS)).wait_recv()
 
         send_x(p, r).wait_recv()
-        arrived = jnp.where(has_before > 0, x_in[p, rows].astype(F32), 0.0)
+        total = stay[p, rows] + jnp.where(core == 1, s_in[p, rows].astype(F32), 0.0)
+        total += jnp.where(has_before > 0, x_in[p, rows].astype(F32), 0.0)
         inside = jnp.logical_and(row + r * ROWS < dim_next, lane < dim_next)
-        out[0, p, 0, rows] = jnp.where(inside, stay[p, rows] + arrived, 0.0).astype(BF16)
+        out[0, p, 0, rows] = jnp.where(inside, total, 0.0).astype(BF16)
 
         @pl.when(jnp.logical_not(last))
         def _():
             send_y(p, r).start()
 
-    turn = jnp.where(first, TURN_FIRST, TURN)
+    turn = jnp.where(first, jnp.where(core == 1, TURN_ONE, TURN_ZERO), TURN)
 
     def work(t, carry):
         k = t - turn
 
-        @pl.when(jnp.logical_and(k >= 0, k < wides))
+        @pl.when(jnp.logical_and(k >= 0, k < 4))
         def _():
             @pl.when(k == 0)
             def _():
                 cover(1)
-                enter(1)
 
             compute(1, k)
 
@@ -194,10 +266,25 @@
         def _():
             finish(0, t)
 
-        return carry
-
-    def first_compute(i, carry):
-        compute(0, i)
+        i = t - LATE
+
+        @pl.when(jnp.logical_and(jnp.logical_not(first), jnp.logical_and(i >= 0, i < wides - 1)))
+        def _():
+            @pl.when(i == 0)
+            def _():
+                for s in range(4):
+                    ket_load(1, s).wait()
+
+            early(1, i)
+
+        return carry
+
+    def first_early(i, carry):
+        early(0, i)
+        return carry
+
+    def first_compute(k, carry):
+        compute(0, k)
         return carry
 
     def last_finish(r, carry):
@@ -206,8 +293,15 @@
 
     cover(0)
     pl.semaphore_wait(barrier, 5)
-    enter(0)
-    lax.fori_loop(0, wides, first_compute, 0)
+
+    @pl.when(jnp.logical_not(first))
+    def _():
+        for s in range(4):
+            ket_load(0, s).wait()
+            bra_load(s).wait()
+        lax.fori_loop(0, wides - 1, first_early, 0)
+
+    lax.fori_loop(0, 4, first_compute, 0)
 
     @pl.when(first)
     def _():
@@ -215,7 +309,8 @@
 
     for s in (3, 1, 2, 0):
         ket_load(1, s).start()
-    lax.fori_loop(0, jnp.maximum(turn + wides, chunks), work, 0)
+
+    lax.fori_loop(0, jnp.maximum(turn + 4, chunks), work, 0)
     lax.fori_loop(0, chunks, last_finish, 0)
 
     def drain(t, carry):
@@ -253,6 +348,7 @@
             pltpu.VMEM(blocks, BF16),
             pltpu.VMEM((4, size, size), BF16),
             pltpu.VMEM((pairs, 4, size, size), BF16),
+            pltpu.VMEM((4, size, size), BF16),
             pltpu.VMEM(blocks, F32),
             pltpu.VMEM((size, size), F32),
             pltpu.VMEM(blocks, BF16),

time: 88.8 us -> 85.8 us (0.966)
  Pallas kernels: 87.7 us -> 84.7 us
    pallas_call x1, Pallas kernels: 87.7 us -> 84.7 us  [per_device(): pl.pallas_call(chain_kernel, out_shape=pltpu.VMEM((1, pairs, 1, size, siz...]
where the time goes in v3:
time: 85.8 us; the launch traced here: 85.7 us
  Pallas kernels  84.7 us (99%)
  local copies, waits for them, and re-layouts  0.97 us (1%)
    pallas_call x1, Pallas kernels, per_device(): pl.pallas_call(chain_kernel, out_shape=pltpu.VMEM((1, pairs, 1, size, siz...  84.7 us

profile of v3, /device:TPU:24, one launch (start us, length us, event | category | flops | bytes accessed | tf_op | source)
XLA Modules:
  0.0 85.7 jit_solution(2433827652628923889)
XLA Ops:
  0.0 84.7 %shard_map.55 = bf16[1,2,1,512,512]{4,3,2,1,0:T(8,128)(2,1)S(1)} custom-call(s32[5,64]{1,0:T(8,128)} %dims.1, s32[1,1,4]{2,1,0:T(1,128)} %bitcast.1, bf16[2,1,512,512]{3,2,1,0:T(8,128)(2,1)} %env.1, bf16[1,4,1,512,512]{4,3,2,1,0:T(8,128)(2,1)} %bra.1, bf16[1,2,4,1,512,512]{5,4,3,2,1,0:T(8,128)(2,1)} %ket.1), custom_call_target="tpu_custom_call" | custom-call | flops 4294967296 | bytes 8388608 | tf_op jit(solution)/shard_map/pallas_call | solution.py:342
  84.7 1.0 %copy.7 = bf16[1,2,1,512,512]{4,3,2,1,0:T(8,128)(2,1)} copy(bf16[1,2,1,512,512]{4,3,2,1,0:T(8,128)(2,1)S(1)} %shard_map.55) | data formatting | bytes 2097152

commit v4 on v3

--- a/solution.py
+++ b/solution.py
@@ -7,10 +7,12 @@
 
 MESH = pl.DeviceIdType.MESH
 WIDE = 128
+HALF = 256
 ROWS = 64
 TURN = 8
-TURN_ZERO = 8
-TURN_ONE = 8
+TURN_ZERO = 3
+TURN_ONE = 4
+RELAYED = 3
 LATE = 5
 F32 = jnp.float32
 BF16 = jnp.bfloat16
@@ -20,6 +22,7 @@
     dims, flags, env, bra, ket, out,
     env_v, bra_v, ket_v, moved, stay, three, s_out, s_in, x_out, x_in,
     env_sem, bra_sem, ket_sem, s_send, s_recv, x_send, x_recv, y_send, y_recv,
+    relay, relay_send, relay_recv,
 ):
     site, sector = lax.axis_index("site"), lax.axis_index("sector")
     sites, sectors = lax.axis_size("site"), lax.axis_size("sector")
@@ -52,17 +55,49 @@
             x_out.at[p, rows], x_in.at[p, rows], x_send.at[p, r], x_recv.at[p, r],
             device_id=(site, ahead), device_id_type=MESH)
 
+    def detour(p, r):
+        sends = (site == 1) if p == 0 else jnp.logical_or(site == 1, site == 2)
+        return jnp.logical_and(jnp.logical_and(core == 1, r < RELAYED), sends)
+
     def send_y(p, r):
         rows = pl.ds(pl.multiple_of(r * ROWS, ROWS), ROWS)
         return pltpu.make_async_remote_copy(
             out.at[0, p, 0, rows], env_v.at[p, rows], y_send.at[p, r], y_recv.at[p, r],
             device_id=(lax.rem(site + 1, sites), sector), device_id_type=MESH)
 
+    def send_relay(p, r):
+        rows = pl.ds(pl.multiple_of(r * ROWS, ROWS), ROWS)
+        return pltpu.make_async_remote_copy(
+            out.at[0, p, 0, rows], relay.at[p, rows], y_send.at[p, r], relay_recv.at[p, r],
+            device_id=(jnp.where(site == 1, 3, 1), jnp.where(site == 1, other, sector)), device_id_type=MESH)
+
+    def send_on(p, r):
+        rows = pl.ds(pl.multiple_of(r * ROWS, ROWS), ROWS)
+        return pltpu.make_async_remote_copy(
+            relay.at[p, rows], env_v.at[p, rows], relay_send.at[p, r], y_recv.at[p, r],
+            device_id=(jnp.where(site == 3, 2, 3), jnp.where(site == 3, other, sector)), device_id_type=MESH)
+
+    def pass_on(p):
+        def body(r, carry):
+            send_relay(p, r).wait_recv()
+            send_on(p, r).start()
+            return carry
+
+        lax.fori_loop(0, RELAYED, body, 0)
+
+    def passed_on(p):
+        def body(r, carry):
+            send_on(p, r).wait_send()
+            return carry
+
+        lax.fori_loop(0, RELAYED, body, 0)
+
     barrier = pltpu.get_barrier_semaphore()
     for partner in (other, ahead, behind):
         pl.semaphore_signal(barrier, inc=1, device_id=(site, partner), device_id_type=MESH)
     for partner in (lax.rem(site + 1, sites), lax.rem(site + sites - 1, sites)):
         pl.semaphore_signal(barrier, inc=1, device_id=(partner, sector), device_id_type=MESH)
+    pl.semaphore_signal(barrier, inc=1, device_id=(lax.rem(site + 2, sites), other), device_id_type=MESH)
 
     @pl.when(first)
     def _():
@@ -114,84 +149,76 @@
         for s in range(4):
             move(p, s, i)
 
-    def rest(p, s):
-        move(p, s, wides - 1)
-
     def part(s, rows):
         return lax.dot_general(bra_v[s, :, rows], moved[s], (((0,), (0,)), ((), ())),
                                preferred_element_type=F32)
 
-    def by_chunk(body):
-        def step(i, carry):
-            body(i, pl.ds(pl.multiple_of(i * WIDE, WIDE), WIDE))
+    def by_half(body):
+        def step(h, carry):
+            body(h, pl.ds(pl.multiple_of(h * HALF, HALF), HALF))
             return carry
 
-        lax.fori_loop(0, wides, step, 0)
+        lax.fori_loop(0, size // HALF, step, 0)
 
     def single(p):
-        def body(i, rows):
+        def body(h, rows):
             s_out[p, rows] = (part(1, rows) + part(2, rows)).astype(BF16)
-            send_s(p, i).start()
-
-        by_chunk(body)
+            for k in range(HALF // WIDE):
+                send_s(p, h * (HALF // WIDE) + k).start()
+
+        by_half(body)
 
     def double(p):
-        rest(p, 3)
-
-        def body(i, rows):
+        def body(h, rows):
             both = part(3, rows)
+            x_out[p, rows] = both.astype(BF16)
+            three[rows] = both
 
             @pl.when(core == 1)
             def _():
-                x_out[p, rows] = both.astype(BF16)
-                for k in range(WIDE // ROWS):
-                    send_x(p, i * (WIDE // ROWS) + k).start()
+                for k in range(HALF // ROWS):
+                    send_x(p, h * (HALF // ROWS) + k).start()
 
             @pl.when(core == 0)
             def _():
-                three[rows] = both
-                x_of(p, i)
-
-        by_chunk(body)
+                for k in range(HALF // WIDE):
+                    x_of(p, h * (HALF // WIDE) + k)
+
+        by_half(body)
 
     def none(p):
-        rest(p, 0)
-
-        def body(i, rows):
+        def body(h, rows):
             stay[p, rows] = part(0, rows)
 
-        by_chunk(body)
+        by_half(body)
 
     def compute_first(p, i):
         rows = pl.ds(pl.multiple_of(i * WIDE, WIDE), WIDE)
         here = env_v[p]
 
-        def whole(s):
-            @pl.when(i == 0)
-            def _():
+        @pl.when(i == 0)
+        def _():
+            for s in (3, 1, 2, 0):
                 if p == 0:
                     bra_load(s).wait()
                 ket_load(p, s).wait()
 
+        def whole(s):
             left = lax.dot_general(bra_v[s, :, rows], here, (((0,), (0,)), ((), ())),
                                    preferred_element_type=F32)
             return dot((left * on[s]).astype(BF16), ket_v[p, s])
 
         both = whole(3)
-
-        @pl.when(core == 1)
-        def _():
-            x_out[p, rows] = both.astype(BF16)
-            for k in range(WIDE // ROWS):
-                send_x(p, i * (WIDE // ROWS) + k).start()
-
-        @pl.when(core == 0)
-        def _():
-            three[rows] = both
-
+        x_out[p, rows] = both.astype(BF16)
+        three[rows] = both
         s_out[p, rows] = (whole(1) + whole(2)).astype(BF16)
+        stay[p, rows] = whole(0)
         send_s(p, i).start()
-        stay[p, rows] = whole(0)
+        if p == 0:
+            @pl.when(core == 1)
+            def _():
+                for k in range(WIDE // ROWS):
+                    send_x(p, i * (WIDE // ROWS) + k).start()
 
         @pl.when(jnp.logical_and(core == 0, i > 0))
         def _():
@@ -205,19 +232,16 @@
         @pl.when(k == 0)
         def _():
             arrive(p, wides - 1)
-
-        @pl.when(jnp.where(core == 1, k == 0, k == 2))
+            for s in (1, 2, 3, 0):
+                move(p, s, wides - 1)
+
+        @pl.when(jnp.where(core == 1, k == 2, k == 1))
+        def _():
+            single(p)
+
+        @pl.when(jnp.where(core == 1, k == 1, k == 2))
         def _():
             double(p)
-
-        @pl.when(jnp.where(core == 1, k == 1, k == 0))
-        def _():
-            rest(p, 1)
-            rest(p, 2)
-
-        @pl.when(jnp.where(core == 1, k == 2, k == 1))
-        def _():
-            single(p)
 
         @pl.when(k == 3)
         def _():
@@ -235,7 +259,11 @@
     def finish(p, r):
         rows = pl.ds(pl.multiple_of(r * ROWS, ROWS), ROWS)
 
-        @pl.when(jnp.logical_and(core == 1, lax.rem(r, WIDE // ROWS) == 0))
+        told = jnp.logical_and(core == 1, lax.rem(r, WIDE // ROWS) == 0)
+        if p == 1:
+            told = jnp.logical_and(told, jnp.logical_not(jnp.logical_and(first, r == 0)))
+
+        @pl.when(told)
         def _():
             send_s(p, r // (WIDE // ROWS)).wait_recv()
 
@@ -245,7 +273,13 @@
         inside = jnp.logical_and(row + r * ROWS < dim_next, lane < dim_next)
         out[0, p, 0, rows] = jnp.where(inside, total, 0.0).astype(BF16)
 
-        @pl.when(jnp.logical_not(last))
+        around = detour(p, r)
+
+        @pl.when(around)
+        def _():
+            send_relay(p, r).start()
+
+        @pl.when(jnp.logical_not(jnp.logical_or(last, around)))
         def _():
             send_y(p, r).start()
 
@@ -292,7 +326,12 @@
         return carry
 
     cover(0)
-    pl.semaphore_wait(barrier, 5)
+    pl.semaphore_wait(barrier, 6)
+
+    @pl.when(jnp.logical_and(site == 3, core == 0))
+    def _():
+        pass_on(0)
+        pass_on(1)
 
     @pl.when(jnp.logical_not(first))
     def _():
@@ -311,7 +350,28 @@
         ket_load(1, s).start()
 
     lax.fori_loop(0, jnp.maximum(turn + 4, chunks), work, 0)
+
+    @pl.when(jnp.logical_and(first, core == 1))
+    def _():
+        send_s(1, 0).wait_recv()
+
+        def send(r, carry):
+            send_x(1, r).start()
+            return carry
+
+        lax.fori_loop(0, chunks, send, 0)
+
     lax.fori_loop(0, chunks, last_finish, 0)
+
+    @pl.when(jnp.logical_and(site == 1, core == 1))
+    def _():
+        pass_on(1)
+        passed_on(1)
+
+    @pl.when(jnp.logical_and(site == 3, core == 0))
+    def _():
+        passed_on(0)
+        passed_on(1)
 
     def drain(t, carry):
         p, r = t // chunks, lax.rem(t, chunks)
@@ -364,6 +424,9 @@
             dma((pairs, chunks)),
             dma((pairs, chunks)),
             dma((pairs, chunks)),
+            pltpu.VMEM((pairs, RELAYED * ROWS, size), BF16),
+            dma((pairs, RELAYED)),
+            dma((pairs, RELAYED)),
         ],
         compiler_params=pltpu.CompilerParams(
             collective_id=0, has_side_effects=True, vmem_limit_bytes=56 << 20

time: 85.8 us -> 83.7 us (0.976)
  Pallas kernels: 84.7 us -> 82.6 us
    pallas_call x1, Pallas kernels: 84.7 us -> 82.6 us  [per_device(): pl.pallas_call(chain_kernel, out_shape=pltpu.VMEM((1, pairs, 1, size, siz...]
where the time goes in v4:
time: 83.7 us; the launch traced here: 83.6 us
  Pallas kernels  82.6 us (99%)
  local copies, waits for them, and re-layouts  0.97 us (1%)
    pallas_call x1, Pallas kernels, per_device(): pl.pallas_call(chain_kernel, out_shape=pltpu.VMEM((1, pairs, 1, size, siz...  82.6 us

profile of v4, /device:TPU:24, one launch (start us, length us, event | category | flops | bytes accessed | tf_op | source)
XLA Modules:
  0.0 83.6 jit_solution(5772956028239531158)
XLA Ops:
  0.0 82.6 %shard_map.55 = bf16[1,2,1,512,512]{4,3,2,1,0:T(8,128)(2,1)S(1)} custom-call(s32[5,64]{1,0:T(8,128)} %dims.1, s32[1,1,4]{2,1,0:T(1,128)} %bitcast.1, bf16[2,1,512,512]{3,2,1,0:T(8,128)(2,1)} %env.1, bf16[1,4,1,512,512]{4,3,2,1,0:T(8,128)(2,1)} %bra.1, bf16[1,2,4,1,512,512]{5,4,3,2,1,0:T(8,128)(2,1)} %ket.1), custom_call_target="tpu_custom_call" | custom-call | flops 4294967296 | bytes 8388608 | tf_op jit(solution)/shard_map/pallas_call | solution.py:402
  82.6 1.0 %copy.7 = bf16[1,2,1,512,512]{4,3,2,1,0:T(8,128)(2,1)} copy(bf16[1,2,1,512,512]{4,3,2,1,0:T(8,128)(2,1)S(1)} %shard_map.55) | data formatting | bytes 2097152

commit v5 on v4

--- a/solution.py
+++ b/solution.py
@@ -10,8 +10,10 @@
 HALF = 256
 ROWS = 64
 TURN = 8
-TURN_ZERO = 3
+TURN_ZERO = 4
 TURN_ONE = 4
+X_FIRST = 6
+X_LAST = 2
 RELAYED = 3
 LATE = 5
 F32 = jnp.float32
@@ -22,7 +24,7 @@
     dims, flags, env, bra, ket, out,
     env_v, bra_v, ket_v, moved, stay, three, s_out, s_in, x_out, x_in,
     env_sem, bra_sem, ket_sem, s_send, s_recv, x_send, x_recv, y_send, y_recv,
-    relay, relay_send, relay_recv,
+    relay, relay_send, relay_recv, x_relay, xr_send, xr_recv,
 ):
     site, sector = lax.axis_index("site"), lax.axis_index("sector")
     sites, sectors = lax.axis_size("site"), lax.axis_size("sector")
@@ -116,12 +118,51 @@
     def dot(a, b):
         return jnp.dot(a, b, preferred_element_type=F32)
 
+    def send_xr(r):
+        rows = pl.ds(pl.multiple_of(r * ROWS, ROWS), ROWS)
+        return pltpu.make_async_remote_copy(
+            x_out.at[1, rows], x_relay.at[rows], x_send.at[1, r], xr_recv.at[r],
+            device_id=(jnp.where(site == 0, 3, 0), sector), device_id_type=MESH)
+
+    def send_xon(r):
+        rows = pl.ds(pl.multiple_of(r * ROWS, ROWS), ROWS)
+        return pltpu.make_async_remote_copy(
+            x_relay.at[rows], x_in.at[1, rows], xr_send.at[r], x_recv.at[1, r],
+            device_id=(jnp.where(site == 0, 3, 0), ahead), device_id_type=MESH)
+
+    def pass_x(count):
+        def body(r, carry):
+            send_xr(r).wait_recv()
+            send_xon(r).start()
+            return carry
+
+        lax.fori_loop(0, count, body, 0)
+
+    def passed_x(count):
+        def body(r, carry):
+            send_xon(r).wait_send()
+            return carry
+
+        lax.fori_loop(0, count, body, 0)
+
     def x_of(p, i):
         send_s(p, i).wait_recv()
         rows = pl.ds(pl.multiple_of(i * WIDE, WIDE), WIDE)
         x_out[p, rows] = (three[rows] + s_in[p, rows].astype(F32)).astype(BF16)
         for k in range(WIDE // ROWS):
-            send_x(p, i * (WIDE // ROWS) + k).start()
+            r = i * (WIDE // ROWS) + k
+            if p == 1:
+                by_site = jnp.logical_and(last, r < X_LAST)
+
+                @pl.when(by_site)
+                def _():
+                    send_xr(r).start()
+
+                @pl.when(jnp.logical_not(by_site))
+                def _():
+                    send_x(p, r).start()
+            else:
+                send_x(p, r).start()
 
     def cover(p):
         @pl.when(first)
@@ -219,6 +260,11 @@
             def _():
                 for k in range(WIDE // ROWS):
                     send_x(p, i * (WIDE // ROWS) + k).start()
+        else:
+            @pl.when(jnp.logical_and(core == 1, i < X_FIRST // (WIDE // ROWS)))
+            def _():
+                for k in range(WIDE // ROWS):
+                    send_xr(i * (WIDE // ROWS) + k).start()
 
         @pl.when(jnp.logical_and(core == 0, i > 0))
         def _():
@@ -322,7 +368,7 @@
         return carry
 
     def last_finish(r, carry):
-        finish(1, r)
+        finish(1, jnp.where(jnp.logical_and(last, core == 0), lax.rem(r + X_LAST, chunks), r))
         return carry
 
     cover(0)
@@ -332,6 +378,10 @@
     def _():
         pass_on(0)
         pass_on(1)
+
+    @pl.when(jnp.logical_and(site == 3, core == 1))
+    def _():
+        pass_x(X_FIRST)
 
     @pl.when(jnp.logical_not(first))
     def _():
@@ -359,7 +409,7 @@
             send_x(1, r).start()
             return carry
 
-        lax.fori_loop(0, chunks, send, 0)
+        lax.fori_loop(X_FIRST, chunks, send, 0)
 
     lax.fori_loop(0, chunks, last_finish, 0)
 
@@ -367,6 +417,15 @@
     def _():
         pass_on(1)
         passed_on(1)
+
+    @pl.when(jnp.logical_and(site == 3, core == 1))
+    def _():
+        passed_x(X_FIRST)
+
+    @pl.when(jnp.logical_and(site == 0, core == 0))
+    def _():
+        pass_x(X_LAST)
+        passed_x(X_LAST)
 
     @pl.when(jnp.logical_and(site == 3, core == 0))
     def _():
@@ -427,6 +486,9 @@
             pltpu.VMEM((pairs, RELAYED * ROWS, size), BF16),
             dma((pairs, RELAYED)),
             dma((pairs, RELAYED)),
+            pltpu.VMEM((max(X_FIRST, X_LAST) * ROWS, size), BF16),
+            dma((max(X_FIRST, X_LAST),)),
+            dma((max(X_FIRST, X_LAST),)),
         ],
         compiler_params=pltpu.CompilerParams(
             collective_id=0, has_side_effects=True, vmem_limit_bytes=56 << 20

time: 83.7 us -> 82.8 us (0.989)
  Pallas kernels: 82.6 us -> 81.7 us
    pallas_call x1, Pallas kernels: 82.6 us -> 81.7 us  [per_device(): pl.pallas_call(chain_kernel, out_shape=pltpu.VMEM((1, pairs, 1, size, siz...]
where the time goes in v5:
time: 82.8 us; the launch traced here: 82.7 us
  Pallas kernels  81.7 us (99%)
  local copies, waits for them, and re-layouts  0.97 us (1%)
    pallas_call x1, Pallas kernels, per_device(): pl.pallas_call(chain_kernel, out_shape=pltpu.VMEM((1, pairs, 1, size, siz...  81.7 us

profile of v5, /device:TPU:24, one launch (start us, length us, event | category | flops | bytes accessed | tf_op | source)
XLA Modules:
  0.0 82.7 jit_solution(10896185399697844552)
XLA Ops:
  0.0 81.7 %shard_map.55 = bf16[1,2,1,512,512]{4,3,2,1,0:T(8,128)(2,1)S(1)} custom-call(s32[5,64]{1,0:T(8,128)} %dims.1, s32[1,1,4]{2,1,0:T(1,128)} %bitcast.1, bf16[2,1,512,512]{3,2,1,0:T(8,128)(2,1)} %env.1, bf16[1,4,1,512,512]{4,3,2,1,0:T(8,128)(2,1)} %bra.1, bf16[1,2,4,1,512,512]{5,4,3,2,1,0:T(8,128)(2,1)} %ket.1), custom_call_target="tpu_custom_call" | custom-call | flops 4294967296 | bytes 8388608 | tf_op jit(solution)/shard_map/pallas_call | solution.py:461
  81.7 1.0 %copy.7 = bf16[1,2,1,512,512]{4,3,2,1,0:T(8,128)(2,1)} copy(bf16[1,2,1,512,512]{4,3,2,1,0:T(8,128)(2,1)S(1)} %shard_map.55) | data formatting | bytes 2097152

commit v6 on v5

--- a/solution.py
+++ b/solution.py
@@ -58,8 +58,7 @@
             device_id=(site, ahead), device_id_type=MESH)
 
     def detour(p, r):
-        sends = (site == 1) if p == 0 else jnp.logical_or(site == 1, site == 2)
-        return jnp.logical_and(jnp.logical_and(core == 1, r < RELAYED), sends)
+        return jnp.logical_and(jnp.logical_and(core == 1, r < RELAYED), site == 1)
 
     def send_y(p, r):
         rows = pl.ds(pl.multiple_of(r * ROWS, ROWS), ROWS)
@@ -71,13 +70,13 @@
         rows = pl.ds(pl.multiple_of(r * ROWS, ROWS), ROWS)
         return pltpu.make_async_remote_copy(
             out.at[0, p, 0, rows], relay.at[p, rows], y_send.at[p, r], relay_recv.at[p, r],
-            device_id=(jnp.where(site == 1, 3, 1), jnp.where(site == 1, other, sector)), device_id_type=MESH)
+            device_id=(3, other), device_id_type=MESH)
 
     def send_on(p, r):
         rows = pl.ds(pl.multiple_of(r * ROWS, ROWS), ROWS)
         return pltpu.make_async_remote_copy(
             relay.at[p, rows], env_v.at[p, rows], relay_send.at[p, r], y_recv.at[p, r],
-            device_id=(jnp.where(site == 3, 2, 3), jnp.where(site == 3, other, sector)), device_id_type=MESH)
+            device_id=(2, other), device_id_type=MESH)
 
     def pass_on(p):
         def body(r, carry):
@@ -412,11 +411,6 @@
         lax.fori_loop(X_FIRST, chunks, send, 0)
 
     lax.fori_loop(0, chunks, last_finish, 0)
-
-    @pl.when(jnp.logical_and(site == 1, core == 1))
-    def _():
-        pass_on(1)
-        passed_on(1)
 
     @pl.when(jnp.logical_and(site == 3, core == 1))
     def _():

time: 82.8 us -> 84.3 us (1.018)
  Pallas kernels: 81.7 us -> 83.2 us
    pallas_call x1, Pallas kernels: 81.7 us -> 83.2 us  [per_device(): pl.pallas_call(chain_kernel, out_shape=pltpu.VMEM((1, pairs, 1, size, siz...]
where the time goes in v6:
time: 84.3 us; the launch traced here: 84.2 us
  Pallas kernels  83.2 us (99%)
  local copies, waits for them, and re-layouts  0.97 us (1%)
    pallas_call x1, Pallas kernels, per_device(): pl.pallas_call(chain_kernel, out_shape=pltpu.VMEM((1, pairs, 1, size, siz...  83.2 us

profile of v6, /device:TPU:24, one launch (start us, length us, event | category | flops | bytes accessed | tf_op | source)
XLA Modules:
  0.0 84.2 jit_solution(6928009631671541162)
XLA Ops:
  0.0 83.2 %shard_map.55 = bf16[1,2,1,512,512]{4,3,2,1,0:T(8,128)(2,1)S(1)} custom-call(s32[5,64]{1,0:T(8,128)} %dims.1, s32[1,1,4]{2,1,0:T(1,128)} %bitcast.1, bf16[2,1,512,512]{3,2,1,0:T(8,128)(2,1)} %env.1, bf16[1,4,1,512,512]{4,3,2,1,0:T(8,128)(2,1)} %bra.1, bf16[1,2,4,1,512,512]{5,4,3,2,1,0:T(8,128)(2,1)} %ket.1), custom_call_target="tpu_custom_call" | custom-call | flops 4294967296 | bytes 8388608 | tf_op jit(solution)/shard_map/pallas_call | solution.py:455
  83.3 1.0 %copy.7 = bf16[1,2,1,512,512]{4,3,2,1,0:T(8,128)(2,1)} copy(bf16[1,2,1,512,512]{4,3,2,1,0:T(8,128)(2,1)S(1)} %shard_map.55) | data formatting | bytes 2097152
